TPU v7x, 512 devices: a whole 4x8x8 slice. The times are simulated.
512 devices in a mesh: dp: 16 (over y, core), prec: 32 (over x, z).
Axes of the slice: x: 4, y: 8, z: 8, core: 2. Of those that a mesh axis runs over, the one named last changes fastest.
Arguments:
- grad_part: bfloat16 [16, 40, 16, 32, 2, 1024], P('dp', None, None, 'prec')
- table: int32 [40], replicated, may hold values from 0 to 95, as said below
- left_root: bfloat16 [96, 1024, 1024], P('prec', 'dp'), as said below
- right_root: bfloat16 [96, 1024, 1024], P('prec', 'dp'), as said below
Outputs:
- left_gram_stats: float32 [96, 1024, 1024], P('prec', 'dp')
- right_gram_stats: float32 [96, 1024, 1024], P('prec', 'dp')
- update: bfloat16 [40, 16, 32, 2, 1024], P(None, 'dp', 'prec')
Inputs may be any that keep to these rules, and one draw needn't show every extreme that they name: `table`: the 40 entries are distinct slots; slot s belongs to owner s // 3 of prec; in every draw some owner holds 3 blocks, and slots 0 and 95 are used. `left_root`: symmetric. `right_root`: symmetric.
All inputs are finite; a program needn't handle non-finite values.
Results may differ from a plain program's by a relative error of at most 0.018.
Values may be sent and summed in bfloat16 or wider, within the bound.
A program may use at most 64 MiB of HBM per device.

v0:
```python
import jax
import jax.numpy as jnp
from jax import lax
from jax.sharding import PartitionSpec as P


def strip_terms(own_strip, left_root, col_start, piece):
    mrows = own_strip.shape[1]
    left_term = jnp.einsum("smk,snk->smn", own_strip, piece, preferred_element_type=jnp.float32)
    own_cols = lax.dynamic_slice_in_dim(piece, col_start, mrows, 2)
    right_acc = jnp.einsum("snm,snk->smk", own_cols, piece, preferred_element_type=jnp.float32)
    half_acc = jnp.einsum("smn,snk->smk", left_root, piece, preferred_element_type=jnp.float32)
    return (left_term, right_acc, half_acc)


def body(grad_part, table, left_root, right_root):
    prec_count = lax.axis_size("prec")
    slot_count = left_root.shape[0]
    mrows = left_root.shape[1]
    order = left_root.shape[2]
    block_count = table.shape[0]
    total_slots = slot_count * prec_count
    col_start = lax.axis_index("dp") * mrows
    slot_index = jnp.arange(total_slots, dtype=jnp.int32)
    selector = (slot_index[:, None] == table[None, :]).astype(jnp.bfloat16)
    summed = lax.psum_scatter(
        grad_part[0].astype(jnp.float32).astype(jnp.bfloat16), "dp", scatter_dimension=1, tiled=True
    )
    flat = summed.reshape(block_count, -1)
    placed = jnp.dot(selector, flat, preferred_element_type=jnp.float32).astype(jnp.bfloat16)
    sent = placed.reshape((total_slots,) + summed.shape[1:])
    owned = lax.all_to_all(sent, "prec", split_axis=0, concat_axis=2, tiled=True)
    own_strip = owned.reshape(slot_count, mrows, order)
    left_acc, right_acc, half_acc = strip_terms(
        own_strip, left_root, col_start, lax.all_gather(own_strip, "dp", axis=1, tiled=True)
    )
    half = half_acc.astype(jnp.bfloat16)
    precond = jnp.einsum(
        "smn,snk->smk",
        half,
        lax.all_gather(right_root, "dp", axis=1, tiled=True),
        preferred_element_type=jnp.float32,
    )
    strip_float = own_strip.astype(jnp.float32)
    grad_square = jnp.sum(strip_float * strip_float, axis=(1, 2))
    prec_square = jnp.sum(precond * precond, axis=(1, 2))
    grad_total, prec_total = lax.psum((grad_square, prec_square), "dp")
    factor = jnp.sqrt(grad_total) / (jnp.sqrt(prec_total) + 1e-06)
    grafted = (precond * factor[:, None, None]).astype(jnp.bfloat16)
    rsub = grad_part.shape[4]
    outgoing = grafted.reshape(slot_count, 1, prec_count, rsub, order)
    returned = lax.all_to_all(outgoing, "prec", split_axis=2, concat_axis=0, tiled=True)
    update = jnp.take(returned, table, axis=0)
    return (left_acc, right_acc, update)


def solution(mesh):
    in_specs = (
        P("dp", None, None, "prec", None, None),
        P(),
        P("prec", "dp", None),
        P("prec", "dp", None),
    )
    out_specs = (P("prec", "dp", None), P("prec", "dp", None), P(None, "dp", "prec", None, None))
    return jax.shard_map(body, mesh=mesh, in_specs=in_specs, out_specs=out_specs, check_vma=False)
```

profile of v0, /device:TPU:1, one launch (start us, length us, event | category | flops | bytes accessed | tf_op | source)
XLA Modules:
  0.0 240.6 jit_solution(7405476864857269336)
XLA Ops:
  7.2 0.0 copy-start
  7.2 0.0 copy-start.3
  7.2 0.0 reduce-scatter.2.cloned.1.call-start
  7.2 4.8 %copy.32 = bf16[1,40,16,1,2,1024]{5,1,4,2,3,0:T(8,128)(2,1)} copy(bf16[1,40,16,1,2,1024]{5,4,3,2,1,0:T(2,128)(2,1)} %param.4) | data formatting | bytes 5242880 | tf_op args[0]
  12.0 0.0 reduce-scatter.2.cloned.1.call-update
  12.0 0.0 all-gather.5.cloned.1.call-start
  12.1 0.7 all-gather.5.cloned.1.call-update
  12.8 0.0 all-gather.3.cloned.1.call-start
  12.8 65.4 %reduce-scatter.2.cloned.1.call-done = bf16[40,1,1,2,1024]{4,0,3,2,1:T(8,128)(2,1)} async-done(((bf16[40,16,1,2,1024]{4,0,3,2,1:T(8,128)(2,1)}), bf16[40,1,1,2,1024]{4,0,3,2,1:T(8,128)(2,1)}) %reduce-scatter.2.cloned.1.call-update) | async-done | bytes 163856 | tf_op jit(solution)/shard_map/reduce_scatter | solution.py:26
  78.3 1.1 copy.20
  79.4 0.0 copy-done.3
  79.4 0.2 convolution_convert_fusion
  79.6 0.3 reshape.35
  79.9 19.2 %all_to_all.33 = bf16[96,1,1,2,1024]{4,3,2,1,0:T(2,128)(2,1)S(1)} all-to-all(bf16[96,1,1,2,1024]{4,3,2,1,0:T(2,128)(2,1)S(1)} %bitcast.37), channel_id=1, replica_groups=mesh['dp'=16,'prec'=32] {'prec'}, dimensions={0} | all-to-all | bytes 786432 | tf_op jit(solution)/shard_map/all_to_all | solution.py:32
  99.1 0.3 copy.33
  99.3 0.9 reshape.36
  100.2 0.0 all-gather.3.cloned.1.call-update
  100.3 0.6 multiply_reduce_fusion.1
  100.9 29.3 %all-gather.5.cloned.1.call-done = bf16[3,1024,1024]{2,1,0:T(8,128)(2,1)} async-done(((bf16[3,64,1024]{2,1,0:T(8,128)(2,1)}), bf16[3,1024,1024]{2,1,0:T(8,128)(2,1)}) %all-gather.5.cloned.1.call-update) | async-done | bytes 6291472 | tf_op jit(solution)/shard_map/all_gather | solution.py:41
  130.3 50.2 %all-gather.3.cloned.1.call-done = bf16[3,1024,1024]{2,1,0:T(8,128)(2,1)} async-done(((bf16[3,64,1024]{2,1,0:T(8,128)(2,1)}), bf16[3,1024,1024]{2,1,0:T(8,128)(2,1)}) %all-gather.3.cloned.1.call-update) | async-done | bytes 6291472 | tf_op jit(solution)/shard_map/all_gather | solution.py:35
  180.5 0.0 copy-done
  180.5 7.0 %multiply_reduce_fusion = (f32[3]{0:T(128)S(1)}, f32[3,64,1024]{2,1,0:T(8,128)S(1)}) fusion(bf16[3,1024,1024]{2,1,0:T(8,128)(2,1)} %all-gather.5.cloned.1.call-done, bf16[3,64,1024]{2,1,0:T(8,128)(2,1)S(1)} %copy-done, bf16[3,1024,1024]{2,1,0:T(8,128)(2,1)} %all-gather.3.cloned.1.call-done), kind=kOutput, calls=%fused_computation.6 | convolution fusion | flops 805896192 | bytes 13762572 | tf_op jit(solution)/shard_map/smn,snk->smk/dot_general | solution.py:38
  187.5 0.0 copy-start.2
  187.5 23.3 %all-reduce = (f32[3]{0:T(128)S(1)}, f32[3]{0:T(128)S(1)}) all-reduce(f32[3]{0:T(128)S(1)} %get-tuple-element.14, f32[3]{0:T(128)S(1)} %multiply_reduce_fusion.1), channel_id=1, replica_groups=mesh['dp'=16,'prec'=32] {'dp'}, use_global_device_ids=true, to_apply=%region_4.0 | all-reduce | flops 6 | bytes 48 | tf_op jit(solution)/shard_map/psum | solution.py:47
  210.8 0.1 multiply_convert_fusion
  211.0 0.2 reshape.37
  211.1 1.0 copy.24
  212.1 9.9 %all-to-all-start.1 = ((bf16[3,1,32,2,1024]{4,3,0,1,2:T(2,128)(2,1)}), bf16[3,1,32,2,1024]{4,3,0,1,2:T(2,128)(2,1)S(1)}, u32[]{:S(2)}, u32[]{:S(2)}) async-start(bf16[3,1,32,2,1024]{4,3,0,1,2:T(2,128)(2,1)} %copy.24), calls=%async_computation.2 | async-start | bytes 786432 | tf_op jit(solution)/shard_map/all_to_all | solution.py:52
  222.1 0.0 copy-start.1
  222.1 5.6 %fusion.1 = f32[3,64,1024]{2,1,0:T(8,128)} fusion(bf16[3,1024,1024]{2,1,0:T(8,128)(2,1)} %all-gather.3.cloned.1.call-done, s32[]{:T(128)S(6)} %select_n.20), kind=kOutput, calls=%fused_computation.8 | convolution fusion | flops 402653184 | bytes 7864324 | tf_op jit(solution)/shard_map/snm,snk->smk/dot_general | solution.py:11
  227.7 0.0 copy-done.2
  227.7 0.0 copy-done.1
  227.7 2.9 %fusion.6 = f32[3,64,1024]{2,1,0:T(8,128)} fusion(bf16[3,64,1024]{2,1,0:T(8,128)(2,1)S(1)} %copy-done.2, bf16[3,1024,1024]{2,1,0:T(8,128)(2,1)S(1)} %copy-done.1), kind=kOutput, calls=%fused_computation.20 | convolution fusion | flops 402653184 | bytes 7471104 | tf_op jit(solution)/shard_map/smk,snk->smn/dot_general | solution.py:9
  230.6 1.7 all-to-all-done.1
  232.3 0.9 gather_fusion
  233.2 0.9 fusion.3
  (5 shorter events, 0.1 us)
Async XLA Ops:
  7.2 173.3 %copy-start = (bf16[3,64,1024]{2,1,0:T(8,128)(2,1)S(1)}, bf16[3,64,1024]{2,1,0:T(8,128)(2,1)}, u32[]{:S(2)}) copy-start(bf16[3,64,1024]{2,1,0:T(8,128)(2,1)} %param.6) | copy-start | bytes 1179652
  7.2 72.2 %copy-start.3 = (s32[40]{0:T(128)S(1)}, s32[40]{0:T(128)}, u32[]{:S(2)}) copy-start(s32[40]{0:T(128)} %param.5) | copy-start | bytes 484
  7.2 71.1 %reduce-scatter.2.cloned.1.call-start = ((), (), s32[]{:S(2)}) async-start(), calls=%async_computation.3 | async-start | bytes 2785280 | tf_op jit(solution)/shard_map/reduce_scatter | solution.py:26
  12.0 118.2 %all-gather.5.cloned.1.call-start = ((), (), s32[]{:S(2)}) async-start(), calls=%async_computation.5 | async-start | bytes 6684672 | tf_op jit(solution)/shard_map/all_gather | solution.py:41
  12.8 167.7 %all-gather.3.cloned.1.call-start = ((), (), s32[]{:S(2)}) async-start(), calls=%async_computation.4 | async-start | bytes 6684672 | tf_op jit(solution)/shard_map/all_gather | solution.py:35
  187.5 40.2 %copy-start.2 = (bf16[3,64,1024]{2,1,0:T(8,128)(2,1)S(1)}, bf16[3,64,1024]{2,1,0:T(8,128)(2,1)}, u32[]{:S(2)}) copy-start(bf16[3,64,1024]{2,1,0:T(8,128)(2,1)} %reshape.36) | copy-start | bytes 1179652
  212.1 20.2 %all-to-all-start.1 = ((bf16[3,1,32,2,1024]{4,3,0,1,2:T(2,128)(2,1)}), bf16[3,1,32,2,1024]{4,3,0,1,2:T(2,128)(2,1)S(1)}, u32[]{:S(2)}, u32[]{:S(2)}) async-start(bf16[3,1,32,2,1024]{4,3,0,1,2:T(2,128)(2,1)} %copy.24), calls=%async_computation.2 | async-start | bytes 786432 | tf_op jit(solution)/shard_map/all_to_all | solution.py:52
  222.1 5.7 %copy-start.1 = (bf16[3,1024,1024]{2,1,0:T(8,128)(2,1)S(1)}, bf16[3,1024,1024]{2,1,0:T(8,128)(2,1)}, u32[]{:S(2)}) copy-start(bf16[3,1024,1024]{2,1,0:T(8,128)(2,1)} %all-gather.3.cloned.1.call-done) | copy-start | bytes 18874372
Sparse Core Ops, SparseCore 0:
  12.2 66.0 reduce-scatter.1
  80.4 49.8 all-gather.4
  133.0 47.4 all-gather.2
where the time goes:
time: 245 us; the launch traced here: 241 us
  waiting for transfers between devices  147 us (60%)
  blocking collectives  42.4 us (17%)
  matrix products  15.8 us (6%)
  between operations  13.9 us (6%)
  starting transfers between devices  10 us (4%)
  local copies, waits for them, and re-layouts  9.4 us (4%)
    reduce_scatter x1, waiting for transfers between devices, body(): lax.psum_scatter(grad_part[0].astype(jnp.float32).astype(jnp.bfloat16), '...  65.4 us
    all_gather x1, waiting for transfers between devices, body(): lax.all_gather(own_strip, 'dp', axis=1, tiled=True)  50.2 us
    all_gather x1, waiting for transfers between devices, body(): lax.all_gather(right_root, 'dp', axis=1, tiled=True)  29.3 us
    psum x1, blocking collectives, body(): grad_total, prec_total = lax.psum((grad_square, prec_square), 'dp')  23.3 us
    all_to_all x1, blocking collectives, body(): lax.all_to_all(sent, 'prec', split_axis=0, concat_axis=2, tiled=True)  19.2 us
    all_to_all x1, starting transfers between devices, body(): lax.all_to_all(outgoing, 'prec', split_axis=2, concat_axis=0, tiled=True)  9.9 us
    dot_general x1, matrix products, body(): jnp.einsum('smn,snk->smk', half, lax.all_gather(right_root, 'dp', axis=1,...  7.02 us
    dot_general x1, matrix products, strip_terms(): jnp.einsum('snm,snk->smk', own_cols, piece, preferred_element_type=jnp.fl...  5.64 us
  transfers between devices with their start and end apart: 4, of which 4 were waited for; matrix products, arithmetic and copies ran while one was open for 5% of the time, Pallas kernels for 0%

commit v1 on v0

v1 whole, which is shorter than its diff:
```python
import jax
import jax.numpy as jnp
from jax import lax
from jax.experimental import pallas as pl
from jax.experimental.pallas import tpu as pltpu
from jax.sharding import PartitionSpec as P

MESH = pl.DeviceIdType.MESH
BF = jnp.bfloat16
F32 = jnp.float32

NY = 8
NDP = 16
NPREC = 32
SL = 3
NB = 40
STRIP = 64
ORDER = 1024
LANES = 128
Q = 16
HALF = NB // 2
SUB = HALF // 2
WIN = 5
TILE = 256
SIGNS = (1, -1)


def kernel(
    inv, table, grad, lroot, rroot, left_hbm, right_hbm, upd_hbm,
    part, sib, ringbuf, summed, slots, got, strip_t, strip_m, gall, wall, rfull,
    half_acc, half, prec_m, outgo, back, norm, norms, left_out, right_out, upd_out,
    part_sem, sib_s, sib_r, rs_s, rs_r, b_s, b_r,
    rr_s, rr_r, rd_s, rd_r, gr_s, gr_r, gd_s, gd_r,
    e_s, e_r, n_s, n_r, out_sem,
):
    d = lax.axis_index("dp")
    p = lax.axis_index("prec")
    y = d // 2
    core = d % 2
    other = 2 * y + (1 - core)

    def wrap(v):
        return (v + 4 * NY) % NY

    def dp_of(chip_y):
        return 2 * chip_y + core

    barrier = pltpu.get_barrier_semaphore()

    @pl.loop(1, NDP)
    def _(i):
        pl.semaphore_signal(barrier, inc=1, device_id=((d + i) % NDP, p), device_id_type=MESH)

    @pl.loop(1, NPREC)
    def _(i):
        pl.semaphore_signal(barrier, inc=1, device_id=(d, (p + i) % NPREC), device_id_type=MESH)

    def local_part(g, t):
        c = wrap(y - SIGNS[g] * (1 + t))
        blocks = pl.ds(g * HALF, HALF)
        return pltpu.make_async_copy(
            grad.at[blocks, 2 * c + core], part.at[c, blocks], part_sem.at[g, t]
        )

    def sib_part(g, t):
        c = wrap(y - SIGNS[g] * (1 + t))
        blocks = pl.ds(g * HALF, HALF)
        return pltpu.make_async_remote_copy(
            src_ref=grad.at[blocks, 2 * c + (1 - core)],
            dst_ref=sib.at[c, blocks],
            send_sem=sib_s.at[g, t],
            recv_sem=sib_r.at[g, t],
            device_id=(other, p),
            device_id_type=MESH,
        )

    for t in range(NY):
        for g in range(2):
            local_part(g, t).start()
    for w in range(WIN):
        cols = pl.ds(pl.multiple_of(wrap(y + w) * LANES, LANES), LANES)
        for s in range(SL):
            wall[s, d, :, w * LANES : (w + 1) * LANES] = rroot[s, :, cols]

    pl.semaphore_wait(barrier, NDP + NPREC - 2)
    for t in range(NY):
        for g in range(2):
            sib_part(g, t).start()

    def hop(buf, ss, rs, s, g, k):
        o = wrap(y - SIGNS[g] * (k - 1))
        rows = pl.ds(0, STRIP) if k < 4 else pl.ds(g * (STRIP // 2), STRIP // 2)
        ref = buf.at[s, dp_of(o), rows]
        return pltpu.make_async_remote_copy(
            src_ref=ref,
            dst_ref=ref,
            send_sem=ss.at[s, g, k - 1],
            recv_sem=rs.at[s, g, k - 1],
            device_id=(dp_of(wrap(y + SIGNS[g])), p),
            device_id_type=MESH,
        )

    def landing(buf, ss, rs, s, g, k):
        o = wrap(y - SIGNS[g] * k)
        rows = pl.ds(0, STRIP) if k < 4 else pl.ds(g * (STRIP // 2), STRIP // 2)
        ref = buf.at[s, dp_of(o), rows]
        return pltpu.make_async_remote_copy(
            src_ref=ref,
            dst_ref=ref,
            send_sem=ss.at[s, g, k - 1],
            recv_sem=rs.at[s, g, k - 1],
            device_id=(dp_of(wrap(y + SIGNS[g])), p),
            device_id_type=MESH,
        )

    def across(buf, ss, rs, s, g, k, mine):
        o = wrap(y - SIGNS[g] * k)
        rows = pl.ds(0, STRIP) if k < 4 else pl.ds(g * (STRIP // 2), STRIP // 2)
        ref = buf.at[s, 2 * o + (core if mine else 1 - core), rows]
        n = 0 if k == 0 else 1 + g * 4 + (k - 1)
        return pltpu.make_async_remote_copy(
            src_ref=ref,
            dst_ref=ref,
            send_sem=ss.at[s, n],
            recv_sem=rs.at[s, n],
            device_id=(other, p),
            device_id_type=MESH,
        )

    def ring_start(buf, rsem, dsem, s):
        for g in range(2):
            hop(buf, *rsem, s, g, 1).start()
        across(buf, *dsem, s, 0, 0, True).start()

    def ring_step(buf, rsem, dsem, s, k):
        for g in range(2):
            landing(buf, *rsem, s, g, k).wait_recv()
            if k < 4:
                hop(buf, *rsem, s, g, k + 1).start()
            across(buf, *dsem, s, g, k, True).start()

    def ring_other(buf, dsem, s, k):
        for g in range(2 if k else 1):
            across(buf, *dsem, s, g, k, False).wait_recv()

    def ring_drain(buf, rsem, dsem, s):
        for k in range(5):
            for g in range(2 if k else 1):
                if k:
                    hop(buf, *rsem, s, g, k).wait_send()
                across(buf, *dsem, s, g, k, True).wait_send()

    RR, RD, GR, GD = (rr_s, rr_r), (rd_s, rd_r), (gr_s, gr_r), (gd_s, gd_r)

    def rs_copy(g, t, u):
        c = wrap(y - SIGNS[g] * (1 + t))
        return pltpu.make_async_remote_copy(
            src_ref=part.at[c, pl.ds(g * HALF + u * SUB, SUB)],
            dst_ref=ringbuf.at[g, t, pl.ds(u * SUB, SUB)],
            send_sem=rs_s.at[g, t, u],
            recv_sem=rs_r.at[g, t, u],
            device_id=(dp_of(wrap(y + SIGNS[g])), p),
            device_id_type=MESH,
        )

    for t in range(NY):
        for u in range(2):
            for g in range(2):
                c = wrap(y - SIGNS[g] * (1 + t))
                if u == 0:
                    local_part(g, t).wait()
                    sib_part(g, t).wait_recv()
                blocks = pl.ds(g * HALF + u * SUB, SUB)
                total = part[c, blocks].astype(F32) + sib[c, blocks].astype(F32)
                if t > 0:
                    rs_copy(g, t - 1, u).wait_recv()
                    total += ringbuf[g, t - 1, pl.ds(u * SUB, SUB)].astype(F32)
                if t < NY - 1:
                    part[c, blocks] = total.astype(BF)
                    rs_copy(g, t, u).start()
                else:
                    summed[blocks] = total.astype(BF)
        if t in (1, 3, 5):
            ring_start(wall, RR, RD, t // 2)
        if t == 6:
            ring_step(wall, RR, RD, 0, 1)
    summed[NB] = jnp.zeros((Q, LANES), BF)

    @pl.loop(0, SL * NPREC, unroll=8)
    def _(s):
        slots[s] = summed[inv[s]]

    def b_copy(to, fro):
        return pltpu.make_async_remote_copy(
            src_ref=slots.at[pl.ds(SL * to, SL)],
            dst_ref=got.at[fro],
            send_sem=b_s,
            recv_sem=b_r,
            device_id=(d, to),
            device_id_type=MESH,
        )

    def b_all():
        ref = got.at[pl.ds(0, NPREC - 1)]
        return pltpu.make_async_remote_copy(
            src_ref=ref, dst_ref=ref, send_sem=b_s, recv_sem=b_r,
            device_id=(other, p), device_id_type=MESH,
        )

    def e_copy(s, to, fro):
        return pltpu.make_async_remote_copy(
            src_ref=outgo.at[s, to],
            dst_ref=back.at[SL * fro + s],
            send_sem=e_s.at[s],
            recv_sem=e_r.at[s],
            device_id=(d, to),
            device_id_type=MESH,
        )

    def e_all(s):
        ref = outgo.at[s, pl.ds(0, NPREC - 1)]
        return pltpu.make_async_remote_copy(
            src_ref=ref, dst_ref=ref, send_sem=e_s.at[s], recv_sem=e_r.at[s],
            device_id=(other, p), device_id_type=MESH,
        )

    def n_copy(s, to, fro):
        return pltpu.make_async_remote_copy(
            src_ref=norm.at[s],
            dst_ref=norms.at[s, fro],
            send_sem=n_s.at[s],
            recv_sem=n_r.at[s],
            device_id=(to, p),
            device_id_type=MESH,
        )

    def n_all(s):
        ref = norms.at[s, pl.ds(0, NDP - 1)]
        return pltpu.make_async_remote_copy(
            src_ref=ref, dst_ref=ref, send_sem=n_s.at[s], recv_sem=n_r.at[s],
            device_id=(other, p), device_id_type=MESH,
        )

    @pl.loop(1, NPREC)
    def _(i):
        b_copy((p + i) % NPREC, p).start()

    got[p] = slots[pl.ds(SL * p, SL)]

    for s in (1, 2):
        ring_step(wall, RR, RD, s, 1)
    for k in (2, 3):
        for s in range(SL):
            ring_step(wall, RR, RD, s, k)

    def own_strip(s):
        rows = got[:, s].astype(F32).reshape(NPREC * Q, LANES)
        strip_t[...] = rows
        square = jnp.sum(jnp.sum(rows * rows, axis=0, keepdims=True), axis=1, keepdims=True)
        norm[s] = jnp.broadcast_to(square, (8, LANES))
        for c in range(8):
            for r in range(2):
                strip_m[c, pl.ds(r, NPREC, stride=2), :] = strip_t[
                    pl.ds(2 * c + r, NPREC, stride=Q), :
                ]
        for c in range(8):
            gall[s, d, :, c * LANES : (c + 1) * LANES] = strip_m[c].astype(BF)

    def whole_root(s, a):
        for b in range(NY):
            w = (b - a) % NY
            if w < WIN:
                block = wall[s, 2 * a : 2 * a + 2, :, w * LANES : (w + 1) * LANES]
                block = block.reshape(LANES, LANES)
            else:
                w = NY - w
                block = wall[s, 2 * b : 2 * b + 2, :, w * LANES : (w + 1) * LANES]
                block = block.reshape(LANES, LANES).T
            rfull[s, a * LANES : (a + 1) * LANES, b * LANES : (b + 1) * LANES] = block

    def chips(k):
        return [wrap(y + k)] if k in (0, 4) else [wrap(y + k), wrap(y - k)]

    def chip_rows(s, k):
        return jnp.concatenate(
            [gall[s, pl.ds(2 * c, 2)].reshape(LANES, ORDER) for c in chips(k)], axis=0
        )

    def add_products(s, k):
        lhs = []
        for c in chips(k):
            here = pl.ds(pl.multiple_of(c * LANES, LANES), LANES)
            mine = pl.ds(pl.multiple_of(y * LANES, LANES), LANES)
            cols = gall[s, pl.ds(2 * c, 2), :, mine].reshape(LANES, LANES).T
            cols = jnp.where(core == 0, cols[:STRIP], cols[STRIP:])
            lhs.append(jnp.concatenate([lroot[s, :, here], cols], axis=0))
        lhs = jnp.concatenate(lhs, axis=1)
        rhs = chip_rows(s, k)
        for n in range(ORDER // TILE):
            tile = slice(n * TILE, (n + 1) * TILE)
            res = jnp.dot(lhs, rhs[:, tile], preferred_element_type=F32)
            if k == 0:
                half_acc[s, :, tile] = res[:STRIP]
                right_out[s, :, tile] = res[STRIP:]
            elif k < 4:
                half_acc[s, :, tile] += res[:STRIP]
                right_out[s, :, tile] += res[STRIP:]
            else:
                half[:, tile] = (half_acc[s, :, tile] + res[:STRIP]).astype(BF)
                right_out[s, :, tile] += res[STRIP:]

    def left_product(s, k):
        res = lax.dot_general(
            gall[s, d], chip_rows(s, k), (((1,), (1,)), ((), ())), preferred_element_type=F32
        )
        for j, c in enumerate(chips(k)):
            here = pl.ds(pl.multiple_of(c * LANES, LANES), LANES)
            left_out[s, :, here] = res[:, j * LANES : (j + 1) * LANES]

    def precondition(s):
        square = jnp.zeros((1, TILE), F32)
        for n in range(ORDER // TILE):
            tile = slice(n * TILE, (n + 1) * TILE)
            pre = jnp.dot(half[...], rfull[s, :, tile], preferred_element_type=F32)
            square += jnp.sum(pre * pre, axis=0, keepdims=True)
            for h in range(TILE // LANES):
                prec_m[n * (TILE // LANES) + h] = pre[:, h * LANES : (h + 1) * LANES]
        norm[s, 0:1, :] = jnp.broadcast_to(jnp.sum(square, axis=1, keepdims=True), (1, LANES))

        @pl.loop(1, NDP)
        def _(i):
            n_copy(s, (d + i) % NDP, d).start()

        norms[s, d] = norm[s]
        for c in range(8):
            for r in range(2):
                strip_t[pl.ds(2 * c + r, NPREC, stride=Q), :] = prec_m[
                    c, pl.ds(r, NPREC, stride=2), :
                ]

    def send_back(s):
        n_all(s).wait_recv()
        total = jnp.sum(norms[s], axis=0)
        factor = jnp.sqrt(total[1:2]) / (jnp.sqrt(total[0:1]) + 1e-06)
        outgo[s] = (strip_t[...] * factor).astype(BF).reshape(NPREC, Q, LANES)

        @pl.loop(1, NPREC)
        def _(i):
            e_copy(s, (p + i) % NPREC, p).start()

        back[SL * p + s] = outgo[s, p]

    def out_copies(s):
        return [
            pltpu.make_async_copy(left_out.at[s], left_hbm.at[s], out_sem.at[0, s]),
            pltpu.make_async_copy(right_out.at[s], right_hbm.at[s], out_sem.at[1, s]),
        ]

    def grams(s, k):
        ring_other(gall, GD, s, k)
        add_products(s, k)
        left_product(s, k)

    def step(s, k):
        ring_step(gall, GR, GD, s, k)

    def finish(s):
        ring_other(gall, GD, s, 4)
        add_products(s, 4)
        precondition(s)
        left_product(s, 4)
        for copy in out_copies(s):
            copy.start()

    b_all().wait_recv()
    own_strip(0)
    ring_start(gall, GR, GD, 0)
    own_strip(1)
    ring_start(gall, GR, GD, 1)
    for s in range(SL):
        ring_step(wall, RR, RD, s, 4)
    step(0, 1)
    own_strip(2)
    ring_start(gall, GR, GD, 2)
    grams(0, 0)
    step(1, 1)
    grams(1, 0)
    grams(0, 1)
    step(0, 2)
    grams(1, 1)
    step(2, 1)
    grams(0, 2)
    grams(2, 0)
    step(1, 2)
    for s in range(SL):
        for k in range(5):
            ring_other(wall, RD, s, k)
    for a in range(4):
        whole_root(0, a)
    step(0, 3)
    grams(2, 1)
    for a in range(4, NY):
        whole_root(0, a)
    step(2, 2)
    grams(1, 2)
    grams(0, 3)
    step(1, 3)
    grams(2, 2)
    for a in range(4):
        whole_root(1, a)
    step(0, 4)
    grams(1, 3)
    finish(0)
    step(2, 3)
    for a in range(4, NY):
        whole_root(1, a)
    send_back(0)
    step(1, 4)
    for a in range(4):
        whole_root(2, a)
    grams(2, 3)
    finish(1)
    step(2, 4)
    for a in range(4, NY):
        whole_root(2, a)
    send_back(1)
    finish(2)

    for s in range(SL):
        ring_drain(wall, RR, RD, s)
        ring_drain(gall, GR, GD, s)
        n_all(s).wait_send()
    for g in range(2):
        for t in range(NY):
            sib_part(g, t).wait_send()
            if t < NY - 1:
                for u in range(2):
                    rs_copy(g, t, u).wait_send()
    b_all().wait_send()
    for s in range(2):
        e_all(s).wait_send()
        e_all(s).wait_recv()
    send_back(2)
    e_all(2).wait_send()
    e_all(2).wait_recv()

    @pl.loop(0, NB, unroll=8)
    def _(b):
        upd_out[b] = back[table[b]]

    last = pltpu.make_async_copy(upd_out, upd_hbm, out_sem.at[2, 0])
    last.start()
    for s in range(SL):
        for copy in out_copies(s):
            copy.wait()
    last.wait()


def hand_over(left_in, right_in, upd_in, left, right, upd, sem):
    copies = [pltpu.make_async_copy(upd_in, upd, sem.at[2, 0])]
    for s in range(SL):
        copies.append(pltpu.make_async_copy(left_in.at[s], left.at[s], sem.at[0, s]))
        copies.append(pltpu.make_async_copy(right_in.at[s], right.at[s], sem.at[1, s]))
    for copy in copies:
        copy.start()
    for copy in copies:
        copy.wait()


def body(grad_part, table, left_root, right_root):
    grad = grad_part.reshape(NB, NDP, 2, 8, LANES).transpose(0, 1, 3, 2, 4)
    grad = grad.reshape(NB, NDP, Q, LANES)
    slot = jnp.arange(SL * NPREC, dtype=jnp.int32)
    block = jnp.arange(NB, dtype=jnp.int32) - NB
    named = slot[:, None] == table[None, :]
    inv = NB + jnp.sum(jnp.where(named, block[None, :], 0), axis=1, dtype=jnp.int32)
    vmem = pl.BlockSpec(memory_space=pltpu.VMEM)
    smem = pl.BlockSpec(memory_space=pltpu.SMEM)
    hbm = pl.BlockSpec(memory_space=pl.ANY)
    dma = pltpu.SemaphoreType.DMA
    results = [
        jax.ShapeDtypeStruct((SL, STRIP, ORDER), F32),
        jax.ShapeDtypeStruct((SL, STRIP, ORDER), F32),
        jax.ShapeDtypeStruct((NB, Q, LANES), BF),
    ]
    out = pl.pallas_call(
        kernel,
        out_shape=results,
        in_specs=[smem, smem, hbm, vmem, vmem],
        out_specs=[hbm, hbm, hbm],
        scratch_shapes=[
            pltpu.VMEM((NY, NB, Q, LANES), BF),
            pltpu.VMEM((NY, NB, Q, LANES), BF),
            pltpu.VMEM((2, NY - 1, HALF, Q, LANES), BF),
            pltpu.VMEM((NB + 1, Q, LANES), BF),
            pltpu.VMEM((SL * NPREC, Q, LANES), BF),
            pltpu.VMEM((NPREC, SL, Q, LANES), BF),
            pltpu.VMEM((NPREC * Q, LANES), F32),
            pltpu.VMEM((8, STRIP, LANES), F32),
            pltpu.VMEM((SL, NDP, STRIP, ORDER), BF),
            pltpu.VMEM((SL, NDP, STRIP, WIN * LANES), BF),
            pltpu.VMEM((SL, ORDER, ORDER), BF),
            pltpu.VMEM((SL, STRIP, ORDER), F32),
            pltpu.VMEM((STRIP, ORDER), BF),
            pltpu.VMEM((8, STRIP, LANES), F32),
            pltpu.VMEM((SL, NPREC, Q, LANES), BF),
            pltpu.VMEM((SL * NPREC, Q, LANES), BF),
            pltpu.VMEM((SL, 8, LANES), F32),
            pltpu.VMEM((SL, NDP, 8, LANES), F32),
            pltpu.VMEM((SL, STRIP, ORDER), F32),
            pltpu.VMEM((SL, STRIP, ORDER), F32),
            pltpu.VMEM((NB, Q, LANES), BF),
            dma((2, NY)), dma((2, NY)), dma((2, NY)),
            dma((2, NY - 1, 2)), dma((2, NY - 1, 2)),
            dma, dma,
            dma((SL, 2, 4)), dma((SL, 2, 4)), dma((SL, 9)), dma((SL, 9)),
            dma((SL, 2, 4)), dma((SL, 2, 4)), dma((SL, 9)), dma((SL, 9)),
            dma((SL,)), dma((SL,)),
            dma((SL,)), dma((SL,)),
            dma((3, SL)),
        ],
        compiler_params=pltpu.CompilerParams(
            collective_id=0, has_side_effects=True, vmem_limit_bytes=56 * 2**20
        ),
        cost_estimate=pl.CostEstimate(
            flops=2 * SL * 5 * STRIP * ORDER * ORDER, bytes_accessed=8 * 2**20, transcendentals=0
        ),
        name="shampoo_step",
    )(inv, table, grad, left_root, right_root)
    left, right, upd = pl.pallas_call(
        hand_over,
        out_shape=results,
        in_specs=[hbm, hbm, hbm],
        out_specs=[hbm, hbm, hbm],
        scratch_shapes=[dma((3, SL))],
        compiler_params=pltpu.CompilerParams(vmem_limit_bytes=56 * 2**20),
        name="hand_over",
    )(*out)
    update = upd.reshape(NB, 8, 2, LANES).transpose(0, 2, 1, 3).reshape(NB, 1, 1, 2, ORDER)
    return (left, right, update)


def solution(mesh):
    in_specs = (
        P("dp", None, None, "prec", None, None),
        P(),
        P("prec", "dp", None),
        P("prec", "dp", None),
    )
    out_specs = (P("prec", "dp", None), P("prec", "dp", None), P(None, "dp", "prec", None, None))
    return jax.shard_map(body, mesh=mesh, in_specs=in_specs, out_specs=out_specs, check_vma=False)
```

time: 245 us -> 169 us (0.69); the launches traced: 241 us -> 168 us
  Pallas kernels: 0 us -> 167 us
  waiting for transfers between devices: 147 us -> 0 us
  blocking collectives: 42.4 us -> 0 us
  matrix products: 15.8 us -> 0 us
  between operations: 13.9 us -> 0.65 us
  starting transfers between devices: 10 us -> 0 us
  local copies, waits for them, and re-layouts: 9.4 us -> 0 us
    pallas_call x0 -> x2, Pallas kernels: none -> 167 us  [the longest x1 113 us: body(): pl.pallas_call(kernel, out_shape=results, in_specs=[smem, smem, hbm, vmem...]
    all_gather x2 -> x0, waiting for transfers between devices: 79.6 us -> none  [the longest x1 50.2 us: body(): lax.all_gather(own_strip, 'dp', axis=1, tiled=True)]
    reduce_scatter x1 -> x0, waiting for transfers between devices: 65.4 us -> none  [body(): lax.psum_scatter(grad_part[0].astype(jnp.float32).astype(jnp.bfloat16), '...]
    psum x1 -> x0, blocking collectives: 23.3 us -> none  [body(): grad_total, prec_total = lax.psum((grad_square, prec_square), 'dp')]
    all_to_all x1 -> x0, blocking collectives: 19.2 us -> none  [body(): lax.all_to_all(sent, 'prec', split_axis=0, concat_axis=2, tiled=True)]
    dot_general x4 -> x0, matrix products: 15.8 us -> none  [the longest x1 7.02 us: body(): jnp.einsum('smn,snk->smk', half, lax.all_gather(right_root, 'dp', axis=1,...]
    all_to_all x1 -> x0, starting transfers between devices: 9.9 us -> none  [body(): lax.all_to_all(outgoing, 'prec', split_axis=2, concat_axis=0, tiled=True)]
    unnamed x10 -> x0, local copies, waits for them, and re-layouts: 4.83 us -> none
  transfers between devices with their start and end apart: 4 -> 0, of which waited for: 4 -> 0; matrix products, arithmetic and copies ran while one was open for 5% -> 0% of each run, Pallas kernels for 0% -> 0%
where the time goes in v1:
time: 169 us; the launch traced here: 168 us
  Pallas kernels  167 us (99%)
    pallas_call x1, Pallas kernels, body(): pl.pallas_call(kernel, out_shape=results, in_specs=[smem, smem, hbm, vmem...  113 us
    pallas_call x1, Pallas kernels, body(): pl.pallas_call(hand_over, out_shape=results, in_specs=[hbm, hbm, hbm], ou...  53.8 us

profile of v1, /device:TPU:1, one launch (start us, length us, event | category | flops | bytes accessed | tf_op | source)
XLA Modules:
  0.0 168.4 jit_solution(15720322284901386665)
XLA Ops:
  0.6 0.7 select_reduce_fusion
  1.4 0.5 broadcast_add_fusion.inv
  1.9 112.7 %shampoo_step.1 = (f32[3,64,1024]{2,1,0:T(8,128)}, f32[3,64,1024]{2,1,0:T(8,128)}, bf16[40,16,128]{2,1,0:T(8,128)(2,1)}) custom-call(s32[96]{0:T(128)} %broadcast_add_fusion.inv, s32[40]{0:T(128)} %table.1, bf16[40,16,16,128]{3,2,1,0:T(8,128)(2,1)} %bitcast.10, bf16[3,64,1024]{2,1,0:T(8,128)(2,1)} %lroot.1, bf16[3,64,1024]{2,1,0:T(8,128)(2,1)} %rroot.1), custom_call_target="tpu_custom_call" | custom-call | flops 2013265920 | bytes 8388608 | tf_op jit(solution)/shard_map/shampoo_step/pallas_call | solution.py:486
  114.6 53.8 %hand_over.1 = (f32[3,64,1024]{2,1,0:T(8,128)}, f32[3,64,1024]{2,1,0:T(8,128)}, bf16[40,16,128]{2,1,0:T(8,128)(2,1)}) custom-call(f32[3,64,1024]{2,1,0:T(8,128)} %get-tuple-element.9.left_in, f32[3,64,1024]{2,1,0:T(8,128)} %get-tuple-element.10.right_in, bf16[40,16,128]{2,1,0:T(8,128)(2,1)} %get-tuple-element.11.upd_in), custom_call_target="tpu_custom_call" | custom-call | tf_op jit(solution)/shard_map/hand_over/pallas_call | solution.py:530
  (1 shorter events, 0.0 us)

commit v2 on v1

--- a/solution.py
+++ b/solution.py
@@ -19,7 +19,6 @@
 LANES = 128
 Q = 16
 HALF = NB // 2
-SUB = HALF // 2
 WIN = 5
 TILE = 256
 SIGNS = (1, -1)
@@ -55,35 +54,40 @@
     def _(i):
         pl.semaphore_signal(barrier, inc=1, device_id=(d, (p + i) % NPREC), device_id_type=MESH)
 
+    def chunk(g, t):
+        return wrap(y + SIGNS[g] * (4 - t))
+
+    def share(g, t):
+        return pl.ds(g * HALF, HALF) if t in (0, 4) else pl.ds(0, NB)
+
     def local_part(g, t):
-        c = wrap(y - SIGNS[g] * (1 + t))
-        blocks = pl.ds(g * HALF, HALF)
+        c = chunk(g, t)
         return pltpu.make_async_copy(
-            grad.at[blocks, 2 * c + core], part.at[c, blocks], part_sem.at[g, t]
+            grad.at[share(g, t), 2 * c + core], part.at[c, share(g, t)], part_sem.at[g, t]
         )
 
     def sib_part(g, t):
-        c = wrap(y - SIGNS[g] * (1 + t))
-        blocks = pl.ds(g * HALF, HALF)
-        return pltpu.make_async_remote_copy(
-            src_ref=grad.at[blocks, 2 * c + (1 - core)],
-            dst_ref=sib.at[c, blocks],
+        c = chunk(g, t)
+        return pltpu.make_async_remote_copy(
+            src_ref=grad.at[share(g, t), 2 * c + (1 - core)],
+            dst_ref=sib.at[c, share(g, t)],
             send_sem=sib_s.at[g, t],
             recv_sem=sib_r.at[g, t],
             device_id=(other, p),
             device_id_type=MESH,
         )
 
-    for t in range(NY):
+    for t in range(5):
         for g in range(2):
             local_part(g, t).start()
+
     for w in range(WIN):
         cols = pl.ds(pl.multiple_of(wrap(y + w) * LANES, LANES), LANES)
         for s in range(SL):
             wall[s, d, :, w * LANES : (w + 1) * LANES] = rroot[s, :, cols]
 
     pl.semaphore_wait(barrier, NDP + NPREC - 2)
-    for t in range(NY):
+    for t in range(5):
         for g in range(2):
             sib_part(g, t).start()
 
@@ -152,39 +156,52 @@
 
     RR, RD, GR, GD = (rr_s, rr_r), (rd_s, rd_r), (gr_s, gr_r), (gd_s, gd_r)
 
-    def rs_copy(g, t, u):
-        c = wrap(y - SIGNS[g] * (1 + t))
-        return pltpu.make_async_remote_copy(
-            src_ref=part.at[c, pl.ds(g * HALF + u * SUB, SUB)],
-            dst_ref=ringbuf.at[g, t, pl.ds(u * SUB, SUB)],
-            send_sem=rs_s.at[g, t, u],
-            recv_sem=rs_r.at[g, t, u],
+    def rs_copy(g, t, h):
+        return pltpu.make_async_remote_copy(
+            src_ref=part.at[chunk(g, t), pl.ds(h * HALF, HALF)],
+            dst_ref=ringbuf.at[g, t, pl.ds(h * HALF, HALF)],
+            send_sem=rs_s.at[g, t, h],
+            recv_sem=rs_r.at[g, t, h],
             device_id=(dp_of(wrap(y + SIGNS[g])), p),
             device_id_type=MESH,
         )
 
-    for t in range(NY):
-        for u in range(2):
-            for g in range(2):
-                c = wrap(y - SIGNS[g] * (1 + t))
-                if u == 0:
-                    local_part(g, t).wait()
-                    sib_part(g, t).wait_recv()
-                blocks = pl.ds(g * HALF + u * SUB, SUB)
-                total = part[c, blocks].astype(F32) + sib[c, blocks].astype(F32)
-                if t > 0:
-                    rs_copy(g, t - 1, u).wait_recv()
-                    total += ringbuf[g, t - 1, pl.ds(u * SUB, SUB)].astype(F32)
-                if t < NY - 1:
-                    part[c, blocks] = total.astype(BF)
-                    rs_copy(g, t, u).start()
-                else:
-                    summed[blocks] = total.astype(BF)
-        if t in (1, 3, 5):
-            ring_start(wall, RR, RD, t // 2)
-        if t == 6:
-            ring_step(wall, RR, RD, 0, 1)
-    summed[NB] = jnp.zeros((Q, LANES), BF)
+    def rs_step(g, t, h):
+        blocks = pl.ds(h * HALF, HALF)
+        c = chunk(g, t)
+        total = part[c, blocks].astype(F32) + sib[c, blocks].astype(F32)
+        if t > 1 or (t == 1 and h == g):
+            rs_copy(g, t - 1, h).wait_recv()
+            total += ringbuf[g, t - 1, blocks].astype(F32)
+        part[c, blocks] = total.astype(BF)
+        rs_copy(g, t, h).start()
+
+    def rs_ready(t):
+        for g in range(2):
+            local_part(g, t).wait()
+            sib_part(g, t).wait_recv()
+
+    ring_start(wall, RR, RD, 0)
+    rs_ready(0)
+    for g in range(2):
+        rs_step(g, 0, g)
+    for t in range(1, 4):
+        rs_ready(t)
+        for g in range(2):
+            rs_step(g, t, 1 - g)
+        for g in range(2):
+            rs_step(g, t, g)
+    ring_start(wall, RR, RD, 1)
+    for h in range(2):
+        local_part(h, 4).wait()
+        sib_part(h, 4).wait_recv()
+        blocks = pl.ds(h * HALF, HALF)
+        total = part[y, blocks].astype(F32) + sib[y, blocks].astype(F32)
+        for g in range(2):
+            rs_copy(g, 3, h).wait_recv()
+            total += ringbuf[g, 3, blocks].astype(F32)
+        summed[pl.ds(1 + h * HALF, HALF)] = total.astype(BF)
+    summed[0] = jnp.zeros((Q, LANES), BF)
 
     @pl.loop(0, SL * NPREC, unroll=8)
     def _(s):
@@ -247,11 +264,7 @@
 
     got[p] = slots[pl.ds(SL * p, SL)]
 
-    for s in (1, 2):
-        ring_step(wall, RR, RD, s, 1)
-    for k in (2, 3):
-        for s in range(SL):
-            ring_step(wall, RR, RD, s, k)
+    ring_start(wall, RR, RD, 2)
 
     def own_strip(s):
         rows = got[:, s].astype(F32).reshape(NPREC * Q, LANES)
@@ -266,17 +279,16 @@
         for c in range(8):
             gall[s, d, :, c * LANES : (c + 1) * LANES] = strip_m[c].astype(BF)
 
-    def whole_root(s, a):
-        for b in range(NY):
-            w = (b - a) % NY
-            if w < WIN:
-                block = wall[s, 2 * a : 2 * a + 2, :, w * LANES : (w + 1) * LANES]
-                block = block.reshape(LANES, LANES)
-            else:
-                w = NY - w
-                block = wall[s, 2 * b : 2 * b + 2, :, w * LANES : (w + 1) * LANES]
-                block = block.reshape(LANES, LANES).T
-            rfull[s, a * LANES : (a + 1) * LANES, b * LANES : (b + 1) * LANES] = block
+    def whole_root(s, k):
+        ring_other(wall, RD, s, k)
+        for a in sorted({k, (NY - k) % NY}):
+            strip = wall[s, pl.ds(2 * wrap(y + a), 2)].reshape(LANES, WIN * LANES)
+            for w in range(WIN):
+                b = (a + w) % NY
+                block = strip[:, w * LANES : (w + 1) * LANES]
+                rfull[s, a * LANES : (a + 1) * LANES, b * LANES : (b + 1) * LANES] = block
+                if 0 < w < WIN - 1:
+                    rfull[s, b * LANES : (b + 1) * LANES, a * LANES : (a + 1) * LANES] = block.T
 
     def chips(k):
         return [wrap(y + k)] if k in (0, 4) else [wrap(y + k), wrap(y - k)]
@@ -319,12 +331,16 @@
 
     def precondition(s):
         square = jnp.zeros((1, TILE), F32)
+        near = [wrap(y + a) for a in range(NY)]
+        lhs = jnp.concatenate(
+            [half[:, pl.ds(pl.multiple_of(c * LANES, LANES), LANES)] for c in near], axis=1
+        )
         for n in range(ORDER // TILE):
             tile = slice(n * TILE, (n + 1) * TILE)
-            pre = jnp.dot(half[...], rfull[s, :, tile], preferred_element_type=F32)
+            pre = jnp.dot(lhs, rfull[s, :, tile], preferred_element_type=F32)
             square += jnp.sum(pre * pre, axis=0, keepdims=True)
             for h in range(TILE // LANES):
-                prec_m[n * (TILE // LANES) + h] = pre[:, h * LANES : (h + 1) * LANES]
+                prec_m[near[n * (TILE // LANES) + h]] = pre[:, h * LANES : (h + 1) * LANES]
         norm[s, 0:1, :] = jnp.broadcast_to(jnp.sum(square, axis=1, keepdims=True), (1, LANES))
 
         @pl.loop(1, NDP)
@@ -372,57 +388,60 @@
         for copy in out_copies(s):
             copy.start()
 
+    for s in range(SL):
+        ring_step(wall, RR, RD, s, 1)
+        whole_root(s, 0)
+    for s in range(SL):
+        ring_step(wall, RR, RD, s, 2)
+        whole_root(s, 1)
+    ring_step(wall, RR, RD, 0, 3)
+    whole_root(0, 2)
     b_all().wait_recv()
     own_strip(0)
     ring_start(gall, GR, GD, 0)
+    ring_step(wall, RR, RD, 1, 3)
+    ring_step(wall, RR, RD, 2, 3)
     own_strip(1)
     ring_start(gall, GR, GD, 1)
+    whole_root(1, 2)
+    own_strip(2)
+    whole_root(2, 2)
+    grams(0, 0)
+    step(0, 1)
+    ring_start(gall, GR, GD, 2)
+    whole_root(0, 3)
+    grams(1, 0)
+    step(1, 1)
+    whole_root(1, 3)
+    grams(0, 1)
+    step(0, 2)
     for s in range(SL):
         ring_step(wall, RR, RD, s, 4)
-    step(0, 1)
-    own_strip(2)
-    ring_start(gall, GR, GD, 2)
-    grams(0, 0)
-    step(1, 1)
-    grams(1, 0)
-    grams(0, 1)
-    step(0, 2)
+    whole_root(2, 3)
     grams(1, 1)
     step(2, 1)
     grams(0, 2)
     grams(2, 0)
     step(1, 2)
-    for s in range(SL):
-        for k in range(5):
-            ring_other(wall, RD, s, k)
-    for a in range(4):
-        whole_root(0, a)
+    whole_root(0, 4)
+    grams(2, 1)
     step(0, 3)
-    grams(2, 1)
-    for a in range(4, NY):
-        whole_root(0, a)
+    grams(1, 2)
     step(2, 2)
-    grams(1, 2)
     grams(0, 3)
+    whole_root(1, 4)
     step(1, 3)
     grams(2, 2)
-    for a in range(4):
-        whole_root(1, a)
     step(0, 4)
     grams(1, 3)
+    step(2, 3)
     finish(0)
-    step(2, 3)
-    for a in range(4, NY):
-        whole_root(1, a)
+    step(1, 4)
+    grams(2, 3)
     send_back(0)
-    step(1, 4)
-    for a in range(4):
-        whole_root(2, a)
-    grams(2, 3)
     finish(1)
     step(2, 4)
-    for a in range(4, NY):
-        whole_root(2, a)
+    whole_root(2, 4)
     send_back(1)
     finish(2)
 
@@ -431,11 +450,12 @@
         ring_drain(gall, GR, GD, s)
         n_all(s).wait_send()
     for g in range(2):
-        for t in range(NY):
+        for t in range(5):
             sib_part(g, t).wait_send()
-            if t < NY - 1:
-                for u in range(2):
-                    rs_copy(g, t, u).wait_send()
+        for t in range(4):
+            for h in range(2):
+                if t or h == g:
+                    rs_copy(g, t, h).wait_send()
     b_all().wait_send()
     for s in range(2):
         e_all(s).wait_send()
@@ -471,9 +491,9 @@
     grad = grad_part.reshape(NB, NDP, 2, 8, LANES).transpose(0, 1, 3, 2, 4)
     grad = grad.reshape(NB, NDP, Q, LANES)
     slot = jnp.arange(SL * NPREC, dtype=jnp.int32)
-    block = jnp.arange(NB, dtype=jnp.int32) - NB
+    block = jnp.arange(1, NB + 1, dtype=jnp.int32)
     named = slot[:, None] == table[None, :]
-    inv = NB + jnp.sum(jnp.where(named, block[None, :], 0), axis=1, dtype=jnp.int32)
+    inv = jnp.sum(jnp.where(named, block[None, :], 0), axis=1, dtype=jnp.int32)
     vmem = pl.BlockSpec(memory_space=pltpu.VMEM)
     smem = pl.BlockSpec(memory_space=pltpu.SMEM)
     hbm = pl.BlockSpec(memory_space=pl.ANY)
@@ -491,7 +511,7 @@
         scratch_shapes=[
             pltpu.VMEM((NY, NB, Q, LANES), BF),
             pltpu.VMEM((NY, NB, Q, LANES), BF),
-            pltpu.VMEM((2, NY - 1, HALF, Q, LANES), BF),
+            pltpu.VMEM((2, 4, NB, Q, LANES), BF),
             pltpu.VMEM((NB + 1, Q, LANES), BF),
             pltpu.VMEM((SL * NPREC, Q, LANES), BF),
             pltpu.VMEM((NPREC, SL, Q, LANES), BF),
@@ -510,8 +530,8 @@
             pltpu.VMEM((SL, STRIP, ORDER), F32),
             pltpu.VMEM((SL, STRIP, ORDER), F32),
             pltpu.VMEM((NB, Q, LANES), BF),
-            dma((2, NY)), dma((2, NY)), dma((2, NY)),
-            dma((2, NY - 1, 2)), dma((2, NY - 1, 2)),
+            dma((2, 5)), dma((2, 5)), dma((2, 5)),
+            dma((2, 4, 2)), dma((2, 4, 2)),
             dma, dma,
             dma((SL, 2, 4)), dma((SL, 2, 4)), dma((SL, 9)), dma((SL, 9)),
             dma((SL, 2, 4)), dma((SL, 2, 4)), dma((SL, 9)), dma((SL, 9)),
@@ -530,7 +550,7 @@
     left, right, upd = pl.pallas_call(
         hand_over,
         out_shape=results,
-        in_specs=[hbm, hbm, hbm],
+        in_specs=[vmem, vmem, vmem],
         out_specs=[hbm, hbm, hbm],
         scratch_shapes=[dma((3, SL))],
         compiler_params=pltpu.CompilerParams(vmem_limit_bytes=56 * 2**20),

time: 169 us -> 113 us (0.67)
  Pallas kernels: 167 us -> 111 us
    pallas_call x1, Pallas kernels: 53.8 us -> 2.66 us  [body(): pl.pallas_call(hand_over, out_shape=results, in_specs=[vmem, vmem, vmem],...]
    pallas_call x1, Pallas kernels: 113 us -> 108 us  [body(): pl.pallas_call(kernel, out_shape=results, in_specs=[smem, smem, hbm, vmem...]
where the time goes in v2:
time: 113 us
  Pallas kernels  111 us (98%)
  other arithmetic  1.26 us (1%)
    pallas_call x1, Pallas kernels, body(): pl.pallas_call(kernel, out_shape=results, in_specs=[smem, smem, hbm, vmem...  108 us
    pallas_call x1, Pallas kernels, body(): pl.pallas_call(hand_over, out_shape=results, in_specs=[vmem, vmem, vmem],...  2.66 us

profile of v2, /device:TPU:1, one launch (start us, length us, event | category | flops | bytes accessed | tf_op | source)
XLA Modules:
  0.0 112.5 jit_solution(14758667481168352552)
XLA Ops:
  0.6 1.3 %select_reduce_fusion.inv = s32[96]{0:T(128)} fusion(s32[40]{0:T(128)S(1)} %iota_add_fusion, s32[40]{0:T(128)} %table.1), kind=kLoop, calls=%fused_computation | loop fusion | flops 11424 | bytes 704 | tf_op jit(solution)/shard_map/reduce_sum | solution.py:496
  1.9 108.0 %shampoo_step.1 = (f32[3,64,1024]{2,1,0:T(8,128)}, f32[3,64,1024]{2,1,0:T(8,128)}, bf16[40,16,128]{2,1,0:T(8,128)(2,1)}) custom-call(s32[96]{0:T(128)} %select_reduce_fusion.inv, s32[40]{0:T(128)} %table.1, bf16[40,16,16,128]{3,2,1,0:T(8,128)(2,1)} %bitcast.10, bf16[3,64,1024]{2,1,0:T(8,128)(2,1)} %lroot.1, bf16[3,64,1024]{2,1,0:T(8,128)(2,1)} %rroot.1), custom_call_target="tpu_custom_call" | custom-call | flops 2013265920 | bytes 8388608 | tf_op jit(solution)/shard_map/shampoo_step/pallas_call | solution.py:506
  109.9 2.7 %hand_over.1 = (f32[3,64,1024]{2,1,0:T(8,128)}, f32[3,64,1024]{2,1,0:T(8,128)}, bf16[40,16,128]{2,1,0:T(8,128)(2,1)}) custom-call(f32[3,64,1024]{2,1,0:T(8,128)} %get-tuple-element.9.left_in, f32[3,64,1024]{2,1,0:T(8,128)} %get-tuple-element.10.right_in, bf16[40,16,128]{2,1,0:T(8,128)(2,1)} %get-tuple-element.11.upd_in), custom_call_target="tpu_custom_call" | custom-call | tf_op jit(solution)/shard_map/hand_over/pallas_call | solution.py:550
  (1 shorter events, 0.0 us)

commit v3 on v2

--- a/solution.py
+++ b/solution.py
@@ -27,10 +27,10 @@
 def kernel(
     inv, table, grad, lroot, rroot, left_hbm, right_hbm, upd_hbm,
     part, sib, ringbuf, summed, slots, got, strip_t, strip_m, gall, wall, rfull,
-    half_acc, half, prec_m, outgo, back, norm, norms, left_out, right_out, upd_out,
+    half_acc, half, prec_m, outgo, back, norm, norms, fac, facs, left_out, right_out, upd_out,
     part_sem, sib_s, sib_r, rs_s, rs_r, b_s, b_r,
     rr_s, rr_r, rd_s, rd_r, gr_s, gr_r, gd_s, gd_r,
-    e_s, e_r, n_s, n_r, out_sem,
+    e_s, e_r, n_s, n_r, f_s, f_r, out_sem,
 ):
     d = lax.axis_index("dp")
     p = lax.axis_index("prec")
@@ -268,13 +268,13 @@
 
     def own_strip(s):
         rows = got[:, s].astype(F32).reshape(NPREC * Q, LANES)
-        strip_t[...] = rows
+        strip_t[s] = rows
         square = jnp.sum(jnp.sum(rows * rows, axis=0, keepdims=True), axis=1, keepdims=True)
         norm[s] = jnp.broadcast_to(square, (8, LANES))
         for c in range(8):
             for r in range(2):
                 strip_m[c, pl.ds(r, NPREC, stride=2), :] = strip_t[
-                    pl.ds(2 * c + r, NPREC, stride=Q), :
+                    s, pl.ds(2 * c + r, NPREC, stride=Q), :
                 ]
         for c in range(8):
             gall[s, d, :, c * LANES : (c + 1) * LANES] = strip_m[c].astype(BF)
@@ -350,21 +350,43 @@
         norms[s, d] = norm[s]
         for c in range(8):
             for r in range(2):
-                strip_t[pl.ds(2 * c + r, NPREC, stride=Q), :] = prec_m[
+                strip_t[s, pl.ds(2 * c + r, NPREC, stride=Q), :] = prec_m[
                     c, pl.ds(r, NPREC, stride=2), :
                 ]
 
-    def send_back(s):
+    def factor(s):
         n_all(s).wait_recv()
         total = jnp.sum(norms[s], axis=0)
-        factor = jnp.sqrt(total[1:2]) / (jnp.sqrt(total[0:1]) + 1e-06)
-        outgo[s] = (strip_t[...] * factor).astype(BF).reshape(NPREC, Q, LANES)
+        return jnp.sqrt(total[1:2]) / (jnp.sqrt(total[0:1]) + 1e-06)
+
+    def send_rows(s, rows):
+        outgo[s] = rows.astype(BF).reshape(NPREC, Q, LANES)
 
         @pl.loop(1, NPREC)
         def _(i):
             e_copy(s, (p + i) % NPREC, p).start()
 
         back[SL * p + s] = outgo[s, p]
+
+    def send_back(s):
+        send_rows(s, strip_t[s] * factor(s))
+
+    def f_copy(to, fro):
+        return pltpu.make_async_remote_copy(
+            src_ref=fac,
+            dst_ref=facs.at[fro],
+            send_sem=f_s,
+            recv_sem=f_r,
+            device_id=(d, to),
+            device_id_type=MESH,
+        )
+
+    def f_all():
+        ref = facs.at[pl.ds(0, NPREC - 1)]
+        return pltpu.make_async_remote_copy(
+            src_ref=ref, dst_ref=ref, send_sem=f_s, recv_sem=f_r,
+            device_id=(other, p), device_id_type=MESH,
+        )
 
     def out_copies(s):
         return [
@@ -402,48 +424,62 @@
     ring_step(wall, RR, RD, 1, 3)
     ring_step(wall, RR, RD, 2, 3)
     own_strip(1)
+    whole_root(1, 2)
+    step(0, 1)
     ring_start(gall, GR, GD, 1)
-    whole_root(1, 2)
     own_strip(2)
+    grams(0, 0)
     whole_root(2, 2)
-    grams(0, 0)
-    step(0, 1)
-    ring_start(gall, GR, GD, 2)
-    whole_root(0, 3)
-    grams(1, 0)
-    step(1, 1)
-    whole_root(1, 3)
-    grams(0, 1)
-    step(0, 2)
     for s in range(SL):
         ring_step(wall, RR, RD, s, 4)
+    step(0, 2)
+    whole_root(0, 3)
+    grams(0, 1)
+    whole_root(0, 4)
+    step(1, 1)
+    grams(1, 0)
+    grams(0, 2)
+    step(0, 3)
+    ring_start(gall, GR, GD, 2)
+    whole_root(1, 3)
+    grams(1, 1)
+    grams(0, 3)
+    step(1, 2)
+    grams(2, 0)
+    step(0, 4)
+    step(2, 1)
+    finish(0)
+    step(1, 3)
+    grams(1, 2)
+    whole_root(1, 4)
+    grams(2, 1)
+    step(2, 2)
+    send_back(0)
+    grams(1, 3)
+    step(1, 4)
+    grams(2, 2)
+    step(2, 3)
+    finish(1)
     whole_root(2, 3)
-    grams(1, 1)
-    step(2, 1)
-    grams(0, 2)
-    grams(2, 0)
-    step(1, 2)
-    whole_root(0, 4)
-    grams(2, 1)
-    step(0, 3)
-    grams(1, 2)
-    step(2, 2)
-    grams(0, 3)
-    whole_root(1, 4)
-    step(1, 3)
-    grams(2, 2)
-    step(0, 4)
-    grams(1, 3)
-    step(2, 3)
-    finish(0)
-    step(1, 4)
+    whole_root(2, 4)
     grams(2, 3)
-    send_back(0)
-    finish(1)
     step(2, 4)
-    whole_root(2, 4)
+    ring_other(gall, GD, 2, 4)
+    add_products(2, 4)
+    precondition(2)
+    send_rows(2, strip_t[2])
     send_back(1)
-    finish(2)
+    left_product(2, 4)
+    for copy in out_copies(2):
+        copy.start()
+    fac[...] = jnp.ones_like(fac)
+    fac[2:3, :] = factor(2)
+
+    @pl.loop(1, NPREC)
+    def _(i):
+        f_copy((p + i) % NPREC, p).start()
+
+    facs[p] = fac[...]
 
     for s in range(SL):
         ring_drain(wall, RR, RD, s)
@@ -457,16 +493,17 @@
                 if t or h == g:
                     rs_copy(g, t, h).wait_send()
     b_all().wait_send()
-    for s in range(2):
+    for s in range(SL):
         e_all(s).wait_send()
         e_all(s).wait_recv()
-    send_back(2)
-    e_all(2).wait_send()
-    e_all(2).wait_recv()
+    f_all().wait_send()
+    f_all().wait_recv()
 
     @pl.loop(0, NB, unroll=8)
     def _(b):
-        upd_out[b] = back[table[b]]
+        slot = table[b]
+        scale = facs[lax.div(slot, SL), pl.ds(lax.rem(slot, SL), 1), :]
+        upd_out[b] = (back[slot].astype(F32) * scale).astype(BF)
 
     last = pltpu.make_async_copy(upd_out, upd_hbm, out_sem.at[2, 0])
     last.start()
@@ -476,14 +513,20 @@
     last.wait()
 
 
-def hand_over(left_in, right_in, upd_in, left, right, upd, sem):
-    copies = [pltpu.make_async_copy(upd_in, upd, sem.at[2, 0])]
+def hand_over(left_in, right_in, upd_in, left, right, upd, a, b, c, sem_in, sem_out):
+    ins, outs = [], []
     for s in range(SL):
-        copies.append(pltpu.make_async_copy(left_in.at[s], left.at[s], sem.at[0, s]))
-        copies.append(pltpu.make_async_copy(right_in.at[s], right.at[s], sem.at[1, s]))
-    for copy in copies:
+        for n, (src, mid, dst) in enumerate(((left_in, a, left), (right_in, b, right))):
+            ins.append(pltpu.make_async_copy(src.at[s], mid.at[s], sem_in.at[n, s]))
+            outs.append(pltpu.make_async_copy(mid.at[s], dst.at[s], sem_out.at[n, s]))
+    ins.append(pltpu.make_async_copy(upd_in, c, sem_in.at[2, 0]))
+    outs.append(pltpu.make_async_copy(c, upd, sem_out.at[2, 0]))
+    for copy in ins:
         copy.start()
-    for copy in copies:
+    for arrive, leave in zip(ins, outs):
+        arrive.wait()
+        leave.start()
+    for copy in outs:
         copy.wait()
 
 
@@ -515,7 +558,7 @@
             pltpu.VMEM((NB + 1, Q, LANES), BF),
             pltpu.VMEM((SL * NPREC, Q, LANES), BF),
             pltpu.VMEM((NPREC, SL, Q, LANES), BF),
-            pltpu.VMEM((NPREC * Q, LANES), F32),
+            pltpu.VMEM((SL, NPREC * Q, LANES), F32),
             pltpu.VMEM((8, STRIP, LANES), F32),
             pltpu.VMEM((SL, NDP, STRIP, ORDER), BF),
             pltpu.VMEM((SL, NDP, STRIP, WIN * LANES), BF),
@@ -527,6 +570,8 @@
             pltpu.VMEM((SL * NPREC, Q, LANES), BF),
             pltpu.VMEM((SL, 8, LANES), F32),
             pltpu.VMEM((SL, NDP, 8, LANES), F32),
+            pltpu.VMEM((8, LANES), F32),
+            pltpu.VMEM((NPREC, 8, LANES), F32),
             pltpu.VMEM((SL, STRIP, ORDER), F32),
             pltpu.VMEM((SL, STRIP, ORDER), F32),
             pltpu.VMEM((NB, Q, LANES), BF),
@@ -537,6 +582,7 @@
             dma((SL, 2, 4)), dma((SL, 2, 4)), dma((SL, 9)), dma((SL, 9)),
             dma((SL,)), dma((SL,)),
             dma((SL,)), dma((SL,)),
+            dma, dma,
             dma((3, SL)),
         ],
         compiler_params=pltpu.CompilerParams(
@@ -550,9 +596,15 @@
     left, right, upd = pl.pallas_call(
         hand_over,
         out_shape=results,
-        in_specs=[vmem, vmem, vmem],
+        in_specs=[hbm, hbm, hbm],
         out_specs=[hbm, hbm, hbm],
-        scratch_shapes=[dma((3, SL))],
+        scratch_shapes=[
+            pltpu.VMEM((SL, STRIP, ORDER), F32),
+            pltpu.VMEM((SL, STRIP, ORDER), F32),
+            pltpu.VMEM((NB, Q, LANES), BF),
+            dma((3, SL)),
+            dma((3, SL)),
+        ],
         compiler_params=pltpu.CompilerParams(vmem_limit_bytes=56 * 2**20),
         name="hand_over",
     )(*out)

time: 113 us -> 108 us (0.956)
  Pallas kernels: 111 us -> 106 us
    pallas_call x1, Pallas kernels: 108 us -> 104 us  [body(): pl.pallas_call(kernel, out_shape=results, in_specs=[smem, smem, hbm, vmem...]
where the time goes in v3:
time: 108 us
  Pallas kernels  106 us (98%)
  other arithmetic  1.26 us (1%)
    pallas_call x1, Pallas kernels, body(): pl.pallas_call(kernel, out_shape=results, in_specs=[smem, smem, hbm, vmem...  104 us
    pallas_call x1, Pallas kernels, body(): pl.pallas_call(hand_over, out_shape=results, in_specs=[hbm, hbm, hbm], ou...  2.29 us

profile of v3, /device:TPU:1, one launch (start us, length us, event | category | flops | bytes accessed | tf_op | source)
XLA Modules:
  0.0 107.9 jit_solution(8981821578634014965)
XLA Ops:
  0.6 1.3 %select_reduce_fusion.inv = s32[96]{0:T(128)} fusion(s32[40]{0:T(128)S(1)} %iota_add_fusion, s32[40]{0:T(128)} %table.1), kind=kLoop, calls=%fused_computation | loop fusion | flops 11424 | bytes 704 | tf_op jit(solution)/shard_map/reduce_sum | solution.py:539
  1.9 103.7 %shampoo_step.1 = (f32[3,64,1024]{2,1,0:T(8,128)}, f32[3,64,1024]{2,1,0:T(8,128)}, bf16[40,16,128]{2,1,0:T(8,128)(2,1)}) custom-call(s32[96]{0:T(128)} %select_reduce_fusion.inv, s32[40]{0:T(128)} %table.1, bf16[40,16,16,128]{3,2,1,0:T(8,128)(2,1)} %bitcast.10, bf16[3,64,1024]{2,1,0:T(8,128)(2,1)} %lroot.1, bf16[3,64,1024]{2,1,0:T(8,128)(2,1)} %rroot.1), custom_call_target="tpu_custom_call" | custom-call | flops 2013265920 | bytes 8388608 | tf_op jit(solution)/shard_map/shampoo_step/pallas_call | solution.py:549
  105.6 2.3 %hand_over.1 = (f32[3,64,1024]{2,1,0:T(8,128)}, f32[3,64,1024]{2,1,0:T(8,128)}, bf16[40,16,128]{2,1,0:T(8,128)(2,1)}) custom-call(f32[3,64,1024]{2,1,0:T(8,128)} %get-tuple-element.9.left_in, f32[3,64,1024]{2,1,0:T(8,128)} %get-tuple-element.10.right_in, bf16[40,16,128]{2,1,0:T(8,128)(2,1)} %get-tuple-element.11.upd_in), custom_call_target="tpu_custom_call" | custom-call | tf_op jit(solution)/shard_map/hand_over/pallas_call | solution.py:596
  (1 shorter events, 0.0 us)

commit v4 on v3

--- a/solution.py
+++ b/solution.py
@@ -39,7 +39,7 @@
     other = 2 * y + (1 - core)
 
     def wrap(v):
-        return (v + 4 * NY) % NY
+        return lax.rem(v + NY, NY)
 
     def dp_of(chip_y):
         return 2 * chip_y + core
@@ -48,11 +48,11 @@
 
     @pl.loop(1, NDP)
     def _(i):
-        pl.semaphore_signal(barrier, inc=1, device_id=((d + i) % NDP, p), device_id_type=MESH)
+        pl.semaphore_signal(barrier, inc=1, device_id=(lax.rem(d + i, NDP), p), device_id_type=MESH)
 
     @pl.loop(1, NPREC)
     def _(i):
-        pl.semaphore_signal(barrier, inc=1, device_id=(d, (p + i) % NPREC), device_id_type=MESH)
+        pl.semaphore_signal(barrier, inc=1, device_id=(d, lax.rem(p + i, NPREC)), device_id_type=MESH)
 
     def chunk(g, t):
         return wrap(y + SIGNS[g] * (4 - t))
@@ -241,36 +241,38 @@
             device_id=(other, p), device_id_type=MESH,
         )
 
-    def n_copy(s, to, fro):
-        return pltpu.make_async_remote_copy(
-            src_ref=norm.at[s],
-            dst_ref=norms.at[s, fro],
-            send_sem=n_s.at[s],
-            recv_sem=n_r.at[s],
+    def n_copy(to, fro):
+        return pltpu.make_async_remote_copy(
+            src_ref=norm,
+            dst_ref=norms.at[fro],
+            send_sem=n_s,
+            recv_sem=n_r,
             device_id=(to, p),
             device_id_type=MESH,
         )
 
-    def n_all(s):
-        ref = norms.at[s, pl.ds(0, NDP - 1)]
-        return pltpu.make_async_remote_copy(
-            src_ref=ref, dst_ref=ref, send_sem=n_s.at[s], recv_sem=n_r.at[s],
+    def n_all():
+        ref = norms.at[pl.ds(0, NDP - 1)]
+        return pltpu.make_async_remote_copy(
+            src_ref=ref, dst_ref=ref, send_sem=n_s, recv_sem=n_r,
             device_id=(other, p), device_id_type=MESH,
         )
 
     @pl.loop(1, NPREC)
     def _(i):
-        b_copy((p + i) % NPREC, p).start()
+        b_copy(lax.rem(p + i, NPREC), p).start()
 
     got[p] = slots[pl.ds(SL * p, SL)]
 
     ring_start(wall, RR, RD, 2)
+
+    norm[...] = jnp.zeros_like(norm)
 
     def own_strip(s):
         rows = got[:, s].astype(F32).reshape(NPREC * Q, LANES)
         strip_t[s] = rows
         square = jnp.sum(jnp.sum(rows * rows, axis=0, keepdims=True), axis=1, keepdims=True)
-        norm[s] = jnp.broadcast_to(square, (8, LANES))
+        norm[8 + s : 9 + s, :] = jnp.broadcast_to(square, (1, LANES))
         for c in range(8):
             for r in range(2):
                 strip_m[c, pl.ds(r, NPREC, stride=2), :] = strip_t[
@@ -341,35 +343,28 @@
             square += jnp.sum(pre * pre, axis=0, keepdims=True)
             for h in range(TILE // LANES):
                 prec_m[near[n * (TILE // LANES) + h]] = pre[:, h * LANES : (h + 1) * LANES]
-        norm[s, 0:1, :] = jnp.broadcast_to(jnp.sum(square, axis=1, keepdims=True), (1, LANES))
-
+        norm[s : s + 1, :] = jnp.broadcast_to(jnp.sum(square, axis=1, keepdims=True), (1, LANES))
+
+    def send_norms():
         @pl.loop(1, NDP)
         def _(i):
-            n_copy(s, (d + i) % NDP, d).start()
-
-        norms[s, d] = norm[s]
+            n_copy(lax.rem(d + i, NDP), d).start()
+
+        norms[d] = norm[...]
+
+    def send_rows(s):
         for c in range(8):
             for r in range(2):
                 strip_t[s, pl.ds(2 * c + r, NPREC, stride=Q), :] = prec_m[
                     c, pl.ds(r, NPREC, stride=2), :
                 ]
-
-    def factor(s):
-        n_all(s).wait_recv()
-        total = jnp.sum(norms[s], axis=0)
-        return jnp.sqrt(total[1:2]) / (jnp.sqrt(total[0:1]) + 1e-06)
-
-    def send_rows(s, rows):
-        outgo[s] = rows.astype(BF).reshape(NPREC, Q, LANES)
+        outgo[s] = strip_t[s].astype(BF).reshape(NPREC, Q, LANES)
 
         @pl.loop(1, NPREC)
         def _(i):
-            e_copy(s, (p + i) % NPREC, p).start()
+            e_copy(s, lax.rem(p + i, NPREC), p).start()
 
         back[SL * p + s] = outgo[s, p]
-
-    def send_back(s):
-        send_rows(s, strip_t[s] * factor(s))
 
     def f_copy(to, fro):
         return pltpu.make_async_remote_copy(
@@ -406,6 +401,9 @@
         ring_other(gall, GD, s, 4)
         add_products(s, 4)
         precondition(s)
+        if s == SL - 1:
+            send_norms()
+        send_rows(s)
         left_product(s, 4)
         for copy in out_copies(s):
             copy.start()
@@ -424,67 +422,59 @@
     ring_step(wall, RR, RD, 1, 3)
     ring_step(wall, RR, RD, 2, 3)
     own_strip(1)
+    ring_start(gall, GR, GD, 1)
     whole_root(1, 2)
+    own_strip(2)
+    whole_root(2, 2)
+    whole_root(0, 3)
     step(0, 1)
-    ring_start(gall, GR, GD, 1)
-    own_strip(2)
-    grams(0, 0)
-    whole_root(2, 2)
+    whole_root(1, 3)
     for s in range(SL):
         ring_step(wall, RR, RD, s, 4)
-    step(0, 2)
-    whole_root(0, 3)
-    grams(0, 1)
-    whole_root(0, 4)
+    grams(0, 0)
+    whole_root(2, 3)
     step(1, 1)
     grams(1, 0)
+    step(0, 2)
+    whole_root(0, 4)
+    grams(0, 1)
+    ring_start(gall, GR, GD, 2)
+    grams(1, 1)
+    step(1, 2)
     grams(0, 2)
     step(0, 3)
-    ring_start(gall, GR, GD, 2)
-    whole_root(1, 3)
-    grams(1, 1)
+    whole_root(1, 4)
+    grams(2, 0)
+    grams(1, 2)
+    step(2, 1)
     grams(0, 3)
-    step(1, 2)
-    grams(2, 0)
+    step(1, 3)
     step(0, 4)
-    step(2, 1)
+    grams(2, 1)
     finish(0)
-    step(1, 3)
-    grams(1, 2)
-    whole_root(1, 4)
-    grams(2, 1)
     step(2, 2)
-    send_back(0)
     grams(1, 3)
     step(1, 4)
     grams(2, 2)
     step(2, 3)
     finish(1)
-    whole_root(2, 3)
     whole_root(2, 4)
     grams(2, 3)
     step(2, 4)
-    ring_other(gall, GD, 2, 4)
-    add_products(2, 4)
-    precondition(2)
-    send_rows(2, strip_t[2])
-    send_back(1)
-    left_product(2, 4)
-    for copy in out_copies(2):
-        copy.start()
-    fac[...] = jnp.ones_like(fac)
-    fac[2:3, :] = factor(2)
+    finish(2)
+    n_all().wait_recv()
+    total = jnp.sum(norms[...], axis=0)
+    fac[...] = jnp.sqrt(total[8:16]) / (jnp.sqrt(total[0:8]) + 1e-06)
 
     @pl.loop(1, NPREC)
     def _(i):
-        f_copy((p + i) % NPREC, p).start()
+        f_copy(lax.rem(p + i, NPREC), p).start()
 
     facs[p] = fac[...]
 
     for s in range(SL):
         ring_drain(wall, RR, RD, s)
         ring_drain(gall, GR, GD, s)
-        n_all(s).wait_send()
     for g in range(2):
         for t in range(5):
             sib_part(g, t).wait_send()
@@ -493,6 +483,7 @@
                 if t or h == g:
                     rs_copy(g, t, h).wait_send()
     b_all().wait_send()
+    n_all().wait_send()
     for s in range(SL):
         e_all(s).wait_send()
         e_all(s).wait_recv()
@@ -568,8 +559,8 @@
             pltpu.VMEM((8, STRIP, LANES), F32),
             pltpu.VMEM((SL, NPREC, Q, LANES), BF),
             pltpu.VMEM((SL * NPREC, Q, LANES), BF),
-            pltpu.VMEM((SL, 8, LANES), F32),
-            pltpu.VMEM((SL, NDP, 8, LANES), F32),
+            pltpu.VMEM((16, LANES), F32),
+            pltpu.VMEM((NDP, 16, LANES), F32),
             pltpu.VMEM((8, LANES), F32),
             pltpu.VMEM((NPREC, 8, LANES), F32),
             pltpu.VMEM((SL, STRIP, ORDER), F32),
@@ -581,7 +572,7 @@
             dma((SL, 2, 4)), dma((SL, 2, 4)), dma((SL, 9)), dma((SL, 9)),
             dma((SL, 2, 4)), dma((SL, 2, 4)), dma((SL, 9)), dma((SL, 9)),
             dma((SL,)), dma((SL,)),
-            dma((SL,)), dma((SL,)),
+            dma, dma,
             dma, dma,
             dma((3, SL)),
         ],

time: 108 us -> 107 us (level)
    pallas_call x1, Pallas kernels: 104 us -> 102 us  [body(): pl.pallas_call(kernel, out_shape=results, in_specs=[smem, smem, hbm, vmem...]
where the time goes in v4:
time: 107 us; the launch traced here: 106 us
  Pallas kernels  105 us (98%)
  other arithmetic  1.26 us (1%)
    pallas_call x1, Pallas kernels, body(): pl.pallas_call(kernel, out_shape=results, in_specs=[smem, smem, hbm, vmem...  102 us
    pallas_call x1, Pallas kernels, body(): pl.pallas_call(hand_over, out_shape=results, in_specs=[hbm, hbm, hbm], ou...  2.29 us

profile of v4, /device:TPU:1, one launch (start us, length us, event | category | flops | bytes accessed | tf_op | source)
XLA Modules:
  0.0 106.4 jit_solution(4035284666058828582)
XLA Ops:
  0.6 1.3 %select_reduce_fusion.inv = s32[96]{0:T(128)} fusion(s32[40]{0:T(128)S(1)} %iota_add_fusion, s32[40]{0:T(128)} %table.1), kind=kLoop, calls=%fused_computation | loop fusion | flops 11424 | bytes 704 | tf_op jit(solution)/shard_map/reduce_sum | solution.py:530
  1.9 102.2 %shampoo_step.1 = (f32[3,64,1024]{2,1,0:T(8,128)}, f32[3,64,1024]{2,1,0:T(8,128)}, bf16[40,16,128]{2,1,0:T(8,128)(2,1)}) custom-call(s32[96]{0:T(128)} %select_reduce_fusion.inv, s32[40]{0:T(128)} %table.1, bf16[40,16,16,128]{3,2,1,0:T(8,128)(2,1)} %bitcast.10, bf16[3,64,1024]{2,1,0:T(8,128)(2,1)} %lroot.1, bf16[3,64,1024]{2,1,0:T(8,128)(2,1)} %rroot.1), custom_call_target="tpu_custom_call" | custom-call | flops 2013265920 | bytes 8388608 | tf_op jit(solution)/shard_map/shampoo_step/pallas_call | solution.py:540
  104.1 2.3 %hand_over.1 = (f32[3,64,1024]{2,1,0:T(8,128)}, f32[3,64,1024]{2,1,0:T(8,128)}, bf16[40,16,128]{2,1,0:T(8,128)(2,1)}) custom-call(f32[3,64,1024]{2,1,0:T(8,128)} %get-tuple-element.9.left_in, f32[3,64,1024]{2,1,0:T(8,128)} %get-tuple-element.10.right_in, bf16[40,16,128]{2,1,0:T(8,128)(2,1)} %get-tuple-element.11.upd_in), custom_call_target="tpu_custom_call" | custom-call | tf_op jit(solution)/shard_map/hand_over/pallas_call | solution.py:587
  (1 shorter events, 0.0 us)

commit v5 on v4

--- a/solution.py
+++ b/solution.py
@@ -91,31 +91,25 @@
         for g in range(2):
             sib_part(g, t).start()
 
-    def hop(buf, ss, rs, s, g, k):
-        o = wrap(y - SIGNS[g] * (k - 1))
-        rows = pl.ds(0, STRIP) if k < 4 else pl.ds(g * (STRIP // 2), STRIP // 2)
-        ref = buf.at[s, dp_of(o), rows]
+    def ring_copy(buf, ss, rs, s, g, k, h, o):
+        ref = buf.at[s, dp_of(o), pl.ds(h * (STRIP // 2), STRIP // 2)]
         return pltpu.make_async_remote_copy(
             src_ref=ref,
             dst_ref=ref,
-            send_sem=ss.at[s, g, k - 1],
-            recv_sem=rs.at[s, g, k - 1],
+            send_sem=ss.at[s, g, k - 1, h],
+            recv_sem=rs.at[s, g, k - 1, h],
             device_id=(dp_of(wrap(y + SIGNS[g])), p),
             device_id_type=MESH,
         )
 
-    def landing(buf, ss, rs, s, g, k):
-        o = wrap(y - SIGNS[g] * k)
-        rows = pl.ds(0, STRIP) if k < 4 else pl.ds(g * (STRIP // 2), STRIP // 2)
-        ref = buf.at[s, dp_of(o), rows]
-        return pltpu.make_async_remote_copy(
-            src_ref=ref,
-            dst_ref=ref,
-            send_sem=ss.at[s, g, k - 1],
-            recv_sem=rs.at[s, g, k - 1],
-            device_id=(dp_of(wrap(y + SIGNS[g])), p),
-            device_id_type=MESH,
-        )
+    def hop(buf, ss, rs, s, g, k, h):
+        return ring_copy(buf, ss, rs, s, g, k, h, wrap(y - SIGNS[g] * (k - 1)))
+
+    def landing(buf, ss, rs, s, g, k, h):
+        return ring_copy(buf, ss, rs, s, g, k, h, wrap(y - SIGNS[g] * k))
+
+    def halves(g, k):
+        return (g, 1 - g) if k < 4 else (g,)
 
     def across(buf, ss, rs, s, g, k, mine):
         o = wrap(y - SIGNS[g] * k)
@@ -132,15 +126,19 @@
         )
 
     def ring_start(buf, rsem, dsem, s):
+        for n in range(2):
+            for g in range(2):
+                hop(buf, *rsem, s, g, 1, halves(g, 1)[n]).start()
+        across(buf, *dsem, s, 0, 0, True).start()
+
+    def ring_step(buf, rsem, dsem, s, k):
+        for n in range(len(halves(0, k))):
+            for g in range(2):
+                h = halves(g, k)[n]
+                landing(buf, *rsem, s, g, k, h).wait_recv()
+                if k < 4 and h in halves(g, k + 1):
+                    hop(buf, *rsem, s, g, k + 1, h).start()
         for g in range(2):
-            hop(buf, *rsem, s, g, 1).start()
-        across(buf, *dsem, s, 0, 0, True).start()
-
-    def ring_step(buf, rsem, dsem, s, k):
-        for g in range(2):
-            landing(buf, *rsem, s, g, k).wait_recv()
-            if k < 4:
-                hop(buf, *rsem, s, g, k + 1).start()
             across(buf, *dsem, s, g, k, True).start()
 
     def ring_other(buf, dsem, s, k):
@@ -150,8 +148,8 @@
     def ring_drain(buf, rsem, dsem, s):
         for k in range(5):
             for g in range(2 if k else 1):
-                if k:
-                    hop(buf, *rsem, s, g, k).wait_send()
+                for h in halves(g, k) if k else ():
+                    hop(buf, *rsem, s, g, k, h).wait_send()
                 across(buf, *dsem, s, g, k, True).wait_send()
 
     RR, RD, GR, GD = (rr_s, rr_r), (rd_s, rd_r), (gr_s, gr_r), (gd_s, gd_r)
@@ -569,8 +567,8 @@
             dma((2, 5)), dma((2, 5)), dma((2, 5)),
             dma((2, 4, 2)), dma((2, 4, 2)),
             dma, dma,
-            dma((SL, 2, 4)), dma((SL, 2, 4)), dma((SL, 9)), dma((SL, 9)),
-            dma((SL, 2, 4)), dma((SL, 2, 4)), dma((SL, 9)), dma((SL, 9)),
+            dma((SL, 2, 4, 2)), dma((SL, 2, 4, 2)), dma((SL, 9)), dma((SL, 9)),
+            dma((SL, 2, 4, 2)), dma((SL, 2, 4, 2)), dma((SL, 9)), dma((SL, 9)),
             dma((SL,)), dma((SL,)),
             dma, dma,
             dma, dma,

time: 107 us -> 107 us (level)
  no operation moved by 1% of the time
where the time goes in v5:
time: 107 us
  Pallas kernels  105 us (98%)
  other arithmetic  1.26 us (1%)
    pallas_call x1, Pallas kernels, body(): pl.pallas_call(kernel, out_shape=results, in_specs=[smem, smem, hbm, vmem...  102 us
    pallas_call x1, Pallas kernels, body(): pl.pallas_call(hand_over, out_shape=results, in_specs=[hbm, hbm, hbm], ou...  2.29 us

profile of v5, /device:TPU:1, one launch (start us, length us, event | category | flops | bytes accessed | tf_op | source)
XLA Modules:
  0.0 106.7 jit_solution(5794871025942915665)
XLA Ops:
  0.6 1.3 %select_reduce_fusion.inv = s32[96]{0:T(128)} fusion(s32[40]{0:T(128)S(1)} %iota_add_fusion, s32[40]{0:T(128)} %table.1), kind=kLoop, calls=%fused_computation | loop fusion | flops 11424 | bytes 704 | tf_op jit(solution)/shard_map/reduce_sum | solution.py:528
  1.9 102.5 %shampoo_step.1 = (f32[3,64,1024]{2,1,0:T(8,128)}, f32[3,64,1024]{2,1,0:T(8,128)}, bf16[40,16,128]{2,1,0:T(8,128)(2,1)}) custom-call(s32[96]{0:T(128)} %select_reduce_fusion.inv, s32[40]{0:T(128)} %table.1, bf16[40,16,16,128]{3,2,1,0:T(8,128)(2,1)} %bitcast.10, bf16[3,64,1024]{2,1,0:T(8,128)(2,1)} %lroot.1, bf16[3,64,1024]{2,1,0:T(8,128)(2,1)} %rroot.1), custom_call_target="tpu_custom_call" | custom-call | flops 2013265920 | bytes 8388608 | tf_op jit(solution)/shard_map/shampoo_step/pallas_call | solution.py:538
  104.4 2.3 %hand_over.1 = (f32[3,64,1024]{2,1,0:T(8,128)}, f32[3,64,1024]{2,1,0:T(8,128)}, bf16[40,16,128]{2,1,0:T(8,128)(2,1)}) custom-call(f32[3,64,1024]{2,1,0:T(8,128)} %get-tuple-element.9.left_in, f32[3,64,1024]{2,1,0:T(8,128)} %get-tuple-element.10.right_in, bf16[40,16,128]{2,1,0:T(8,128)(2,1)} %get-tuple-element.11.upd_in), custom_call_target="tpu_custom_call" | custom-call | tf_op jit(solution)/shard_map/hand_over/pallas_call | solution.py:585
  (1 shorter events, 0.0 us)
